TPU v7x, 32 devices: a whole 2x2x4 slice. The times are simulated.
32 devices in a mesh: grp: 2 (over x), gx: 8 (over z, y), yz: 2 (over core).
Axes of the slice: x: 2, y: 2, z: 4, core: 2. Of those that a mesh axis runs over, the one named last changes fastest.
Arguments:
- start: float32 [2, 2, 3, 32, 128, 128], P(None, None, None, ('grp', 'gx'), 'yz'), parts along dimension 3, may hold values from -6 to 6
- masses: float32 [2, 32, 128, 128], P(None, ('grp', 'gx'), 'yz'), parts along dimension 1, may hold values from 0.8 to 1.25
- bond_long: float32 [4, 32, 128, 128], P(None, ('grp', 'gx'), 'yz'), parts along dimension 1, may hold values from 0.5 to 1.5
- bond_trans: float32 [4, 32, 128, 128], P(None, ('grp', 'gx'), 'yz'), parts along dimension 1, may hold values from 0.1 to 0.5
Outputs:
- last_vector: float32 [2, 2, 3, 32, 128, 128], P(None, None, None, ('grp', 'gx'), 'yz'), parts along dimension 3
- density: float32 [4, 2, 32, 128, 128], P(None, None, ('grp', 'gx'), 'yz'), parts along dimension 2
There are 2 independent parts, one for each index of `grp`. A program takes and returns all parts, laid end to end along the dimension named above; each array names one. Nothing has to cross between parts.
All inputs are finite; a program needn't handle non-finite values.
Results may differ from a plain program's by a relative error of at most 0.0001.
Values sent between devices are 32-bit elements; how exact they have to be, the bound alone decides.
A program may use at most 64 MiB of HBM per device.

v0:
```python
import jax
import jax.numpy as jnp
from jax import lax
from jax.sharding import PartitionSpec as P

STEPS = 4


root_third = 0.5773502691896258
bond_signs = [[1.0, 1.0, 1.0], [1.0, -1.0, -1.0], [-1.0, 1.0, -1.0], [-1.0, -1.0, 1.0]]
width_scale = 8.0


def passed_along(block, axis, distance):
    devices = range(lax.axis_size(axis))
    route = [((i - distance) % len(devices), i) for i in devices]
    return lax.ppermute(block, axis, route)


def bond_force(diff, stiff_long, stiff_trans, which):
    signs = bond_signs[which]
    along = (diff[:, 0] * signs[0] + diff[:, 1] * signs[1] + diff[:, 2] * signs[2]) * root_third
    extra = (stiff_long - stiff_trans) * along
    parts = [extra * (signs[comp] * root_third) for comp in range(3)]
    return stiff_trans * diff + jnp.stack(parts, axis=1)


def operate_sending(field, scale, bond_long, bond_trans):
    moved = field * scale[None, :, None]
    upper_a = moved[:, 0]
    upper_b = moved[:, 1]
    force_a = jnp.zeros_like(upper_a)
    force_b = jnp.zeros_like(upper_b)
    for which in range(4):
        if which == 0:
            lower = upper_b
        elif which == 1:
            plane = passed_along(upper_b[:, :, -1:], "gx", 1)
            lower = jnp.concatenate([plane, upper_b[:, :, :-1]], axis=2)
        elif which == 2:
            plane = passed_along(upper_b[:, :, :, -1:], "yz", 1)
            lower = jnp.concatenate([plane, upper_b[:, :, :, :-1]], axis=3)
        else:
            lower = jnp.roll(upper_b, 1, axis=4)
        term = bond_force(upper_a - lower, bond_long[which], bond_trans[which], which)
        force_a = force_a + term
        if which == 0:
            shifted = term
        elif which == 1:
            plane = passed_along(term[:, :, :1], "gx", -1)
            shifted = jnp.concatenate([term[:, :, 1:], plane], axis=2)
        elif which == 2:
            plane = passed_along(term[:, :, :, :1], "yz", -1)
            shifted = jnp.concatenate([term[:, :, :, 1:], plane], axis=3)
        else:
            shifted = jnp.roll(term, -1, axis=4)
        force_b = force_b - shifted
    forces = jnp.stack([force_a, force_b], axis=1)
    return forces * scale[None, :, None] / width_scale - field


def on_device(start, masses, bond_long, bond_trans):
    scale = 1.0 / jnp.sqrt(masses)

    def operate(field):
        return operate_sending(field, scale, bond_long, bond_trans)

    before = start
    current = operate(start)
    moments = [jnp.sum(start * current, axis=(0, 2))]
    for order in range(2, STEPS + 1):
        following = 2.0 * operate(current) - before
        before = current
        current = following
        moments.append(jnp.sum(start * current, axis=(0, 2)))
    return (current, jnp.stack(moments))


def solution(mesh):
    in_specs = (
        P(None, None, None, ("grp", "gx"), "yz", None),
        P(None, ("grp", "gx"), "yz", None),
        P(None, ("grp", "gx"), "yz", None),
        P(None, ("grp", "gx"), "yz", None),
    )
    out_specs = (
        P(None, None, None, ("grp", "gx"), "yz", None),
        P(None, None, ("grp", "gx"), "yz", None),
    )
    return jax.shard_map(
        on_device, mesh=mesh, in_specs=in_specs, out_specs=out_specs, check_vma=False
    )
```

profile of v0, /device:TPU:0, one launch (start us, length us, event | category | flops | bytes accessed | tf_op | source)
XLA Modules:
  0.0 124.9 jit_solution(17402071205004658747)
XLA Ops:
  0.6 0.9 sqrt.3
  1.6 1.2 copy_multiply_fusion.3
  3.4 0.9 slice_bitcast_fusion.27
  4.3 2.5 %collective-permute-start = (f32[2,3,1,64,128]{4,3,0,1,2:T(8,128)}, f32[2,3,1,64,128]{4,3,0,1,2:T(8,128)}, u32[]{:S(2)}, u32[]{:S(2)}) collective-permute-start(f32[2,3,1,64,128]{4,3,0,1,2:T(8,128)} %get-tuple-element.116), channel_id=1, source_target_pairs={{14,0},{0,2},{2,4},{4,6},{6,8},{8,10},{10,12},{12,14},{15,1},{1,3}... | collective-permute-start | bytes 589832 | tf_op jit(solution)/shard_map/ppermute | solution.py:17
  9.2 1.0 copy.554
  10.2 5.5 %collective-permute-done = f32[2,3,1,64,128]{4,3,0,1,2:T(8,128)} collective-permute-done((f32[2,3,1,64,128]{4,3,0,1,2:T(8,128)}, f32[2,3,1,64,128]{4,3,0,1,2:T(8,128)}, u32[]{:S(2)}, u32[]{:S(2)}) %collective-permute-start) | collective-permute-done | bytes 196640 | tf_op jit(solution)/shard_map/ppermute | solution.py:17
  15.7 1.3 %broadcast_multiply_fusion.3 = (f32[2,3,2,64,128]{4,3,0,2,1:T(8,128)S(1)}, f32[2,3,2,64,128]{4,3,0,2,1:T(8,128)S(1)}, f32[2,3,2,64,128]{4,3,0,2,1:T(8,128)S(1)}, f32[2,3,2,64,128]{4,3,0,2,1:T(8,128)S(1)}) fusion(f32[2,64,128]{2,1,0:T(8,128)S(1)} %get-tuple-element.123, f32[2,1,3,2,64,128]{5,4,0,2,3,1:T(8,128)S(1)} %get-tuple-element.63, ...), kind=kLoop, calls=%fused_computation.164 | loop fusion | flops 688128 | bytes 3211264 | tf_op jit(solution)/shard_map/mul | solution.py:25
  22.0 1.7 %collective-permute-start.2 = (f32[2,3,1,64,128]{4,3,0,2,1:T(8,128)}, f32[2,3,1,64,128]{4,3,0,2,1:T(8,128)}, u32[]{:S(2)}, u32[]{:S(2)}) collective-permute-start(f32[2,3,1,64,128]{4,3,0,2,1:T(8,128)} %get-tuple-element.120), channel_id=1, source_target_pairs={{2,0},{4,2},{6,4},{8,6},{10,8},{12,10},{14,12},{0,14},{3,1},{5,3},... | collective-permute-start | bytes 589832 | tf_op jit(solution)/shard_map/ppermute | solution.py:17
  24.4 5.2 %collective-permute-done.2 = f32[2,3,1,64,128]{4,3,0,2,1:T(8,128)} collective-permute-done((f32[2,3,1,64,128]{4,3,0,2,1:T(8,128)}, f32[2,3,1,64,128]{4,3,0,2,1:T(8,128)}, u32[]{:S(2)}, u32[]{:S(2)}) %collective-permute-start.2) | collective-permute-done | bytes 196640 | tf_op jit(solution)/shard_map/ppermute | solution.py:17
  29.6 1.3 %fusion.23 = (f32[2,1,3,2,64,128]{5,4,0,2,3,1:T(8,128)S(1)}, f32[2,1,3,2,64,128]{5,4,0,2,3,1:T(8,128)S(1)}) fusion(f32[2,1,3,1,64,128]{5,4,0,2,3,1:T(8,128)} %bitcast.28, f32[2,1,3,1,64,128]{5,4,0,2,3,1:T(8,128)} %get-tuple-element.119, f32[2,1,3,2,1,128]{5,4,0,2,3,1:T(1,128)} %bitcast.116, f32[2,1,3,2,63,128]{5,4,0,2,3,1:T(8,128)S(1)} %slice_bitcast_fusion.9, ...), kind=kLoop, calls=%fused_computation.54 | loop fusion | flops 786432 | bytes 2555904 | tf_op jit(solution)/shard_map/sub | solution.py:57
  32.3 1.4 %fusion.18 = f32[2,1,3,2,64,128]{5,4,0,3,2,1:T(8,128)S(1)} fusion(f32[2,1,3,1,64,128]{5,4,0,3,2,1:T(8,128)S(1)} %copy-done.31, f32[2,1,3,1,64,128]{5,4,0,3,2,1:T(8,128)} %bitcast.8, f32[2,1,1,2,64,128]{5,4,0,3,2,1:T(8,128)S(1)} %copy-done.40, f32[2,1,1,2,64,128]{5,4,0,3,2,1:T(8,128)S(1)} %copy-done.39, f32[2,1,3,2,63,128]{5,4,0,3,2,1:T(8,128)S(1)} %copy_bitcast_fusion.1, ...), kind=kLoop, calls=%fused_computation.42 | loop fusion | flops 2064384 | bytes 3342336 | tf_op jit(solution)/shard_map/add | solution.py:46
  34.7 1.0 slice_bitcast_fusion.33
  35.6 1.0 slice_bitcast_fusion.32
  36.7 0.9 slice_bitcast_fusion.26
  37.9 1.0 copy.589
  38.9 9.0 %collective-permute-done.4 = f32[2,3,1,64,128]{4,3,0,1,2:T(8,128)} collective-permute-done((f32[2,3,1,64,128]{4,3,0,1,2:T(8,128)}, f32[2,3,1,64,128]{4,3,0,1,2:T(8,128)}, u32[]{:S(2)}, u32[]{:S(2)}) %collective-permute-start.4) | collective-permute-done | bytes 196640 | tf_op jit(solution)/shard_map/ppermute | solution.py:17
  47.9 1.3 %broadcast_multiply_fusion.5 = (f32[2,3,2,64,128]{4,3,0,2,1:T(8,128)S(1)}, f32[2,3,2,64,128]{4,3,0,2,1:T(8,128)S(1)}, f32[2,3,2,64,128]{4,3,0,2,1:T(8,128)S(1)}) fusion(f32[2,64,128]{2,1,0:T(8,128)S(1)} %get-tuple-element.122, f32[2,2,3,2,64,128]{5,4,0,3,2,1:T(8,128)S(1)} %broadcast_multiply_fusion, f32[2,3,2,63,128]{4,3,0,2,1:T(8,128)} %get-tuple-element.106, ...), kind=kLoop, calls=%fused_computation.166 | loop fusion | flops 491520 | bytes 2424832 | tf_op jit(solution)/shard_map/mul | solution.py:25
  49.4 1.8 %collective-permute-start.6 = (f32[2,3,1,64,128]{4,3,0,1,2:T(8,128)S(1)}, f32[2,3,1,64,128]{4,3,0,1,2:T(8,128)S(1)}, u32[]{:S(2)}, u32[]{:S(2)}) collective-permute-start(f32[2,3,1,64,128]{4,3,0,1,2:T(8,128)S(1)} %get-tuple-element.110), channel_id=1, source_target_pairs={{2,0},{4,2},{6,4},{8,6},{10,8},{12,10},{14,12},{0,14},{3,1},{5,3},... | collective-permute-start | bytes 589832 | tf_op jit(solution)/shard_map/ppermute | solution.py:17
  51.5 1.1 collective-permute-done.7
  52.6 3.4 %collective-permute-done.6 = f32[2,3,1,64,128]{4,3,0,1,2:T(8,128)S(1)} collective-permute-done((f32[2,3,1,64,128]{4,3,0,1,2:T(8,128)S(1)}, f32[2,3,1,64,128]{4,3,0,1,2:T(8,128)S(1)}, u32[]{:S(2)}, u32[]{:S(2)}) %collective-permute-start.6) | collective-permute-done | bytes 196640 | tf_op jit(solution)/shard_map/ppermute | solution.py:17
  56.1 0.9 copy-done.23
  58.8 1.4 %fusion.27 = f32[2,1,3,2,64,128]{5,4,0,3,2,1:T(8,128)S(1)} fusion(f32[2,1,1,2,64,128]{5,4,0,3,2,1:T(8,128)S(1)} %get-tuple-element.148, f32[2,1,1,2,64,128]{5,4,0,3,2,1:T(8,128)S(1)} %get-tuple-element.36, f32[2,1,3,2,63,128]{5,4,0,3,2,1:T(8,128)S(1)} %copy-done.18, f32[2,1,3,2,1,128]{5,4,0,3,2,1:T(1,128)S(1)} %bitcast.287, ...), kind=kLoop, calls=%fused_computation.64 | loop fusion | flops 2359296 | bytes 3932160 | tf_op jit(solution)/shard_map/add | solution.py:46
  61.2 0.9 slice_bitcast_fusion.25
  62.1 1.0 slice_bitcast_fusion.30
  63.1 1.0 slice_bitcast_fusion.31
  64.8 0.9 slice.543
  65.7 1.2 copy.620
  66.8 1.0 copy.621
  67.8 6.6 %collective-permute-done.8 = f32[2,3,1,64,128]{4,3,0,1,2:T(8,128)} collective-permute-done((f32[2,3,1,64,128]{4,3,0,1,2:T(8,128)}, f32[2,3,1,64,128]{4,3,0,1,2:T(8,128)}, u32[]{:S(2)}, u32[]{:S(2)}) %collective-permute-start.8) | collective-permute-done | bytes 196640 | tf_op jit(solution)/shard_map/ppermute | solution.py:17
  74.4 3.0 %fusion.33 = (f32[2,1,3,2,64,128]{5,4,0,2,3,1:T(8,128)}, f32[2,1,3,2,64,128]{5,4,0,2,3,1:T(8,128)}, f32[2,1,3,2,64,128]{5,4,0,2,3,1:T(8,128)}, f32[2,1,3,2,64,128]{5,4,0,2,3,1:T(8,128)}, f32[2,3,2,64,128]{4,3,0,1,2:T(8,128)S(1)}) fusion(f32[2,1,3,1,64,128]{5,4,0,2,3,1:T(8,128)} %get-tuple-element.88, f32[2,1,3,1,64,128]{5,4,0,2,3,1:T(8,128)} %bitcast.64, ...), kind=kLoop, calls=%fused_computation.80 | loop fusion | flops 1081344 | bytes 4259840 | tf_op jit(solution)/shard_map/mul | solution.py:25
  77.5 1.2 copy_subtract_fusion.7
  85.3 1.7 %collective-permute-start.10 = (f32[2,3,1,64,128]{4,3,0,2,1:T(8,128)}, f32[2,3,1,64,128]{4,3,0,2,1:T(8,128)}, u32[]{:S(2)}, u32[]{:S(2)}) collective-permute-start(f32[2,3,1,64,128]{4,3,0,2,1:T(8,128)} %get-tuple-element.96), channel_id=1, source_target_pairs={{2,0},{4,2},{6,4},{8,6},{10,8},{12,10},{14,12},{0,14},{3,1},{5,3},... | collective-permute-start | bytes 589832 | tf_op jit(solution)/shard_map/ppermute | solution.py:17
  87.1 0.9 slice_bitcast_fusion.3
  88.2 1.0 copy.631
  89.1 3.8 %collective-permute-done.10 = f32[2,3,1,64,128]{4,3,0,2,1:T(8,128)} collective-permute-done((f32[2,3,1,64,128]{4,3,0,2,1:T(8,128)}, f32[2,3,1,64,128]{4,3,0,2,1:T(8,128)}, u32[]{:S(2)}, u32[]{:S(2)}) %collective-permute-start.10) | collective-permute-done | bytes 196640 | tf_op jit(solution)/shard_map/ppermute | solution.py:17
  92.9 2.5 %fusion.36 = (f32[2,1,3,2,64,128]{5,4,0,3,2,1:T(8,128)S(1)}, f32[2,1,3,2,64,128]{5,4,0,3,2,1:T(8,128)S(1)}) fusion(f32[2,1,1,2,64,128]{5,4,0,3,2,1:T(8,128)} %get-tuple-element.139, f32[2,1,1,2,64,128]{5,4,0,3,2,1:T(8,128)} %get-tuple-element.30, f32[2,1,1,2,64,128]{5,4,0,3,2,1:T(8,128)} %get-tuple-element.136, ...), kind=kLoop, calls=%fused_computation.85 | loop fusion | flops 1966080 | bytes 4390912 | tf_op jit(solution)/shard_map/add | solution.py:46
  97.5 0.9 slice_bitcast_fusion.19
  98.4 1.0 slice_bitcast_fusion.28
  99.4 1.0 slice_bitcast_fusion.29
  100.5 1.0 copy.661
  101.5 1.1 fusion.50
  102.6 9.1 %collective-permute-done.12 = f32[2,3,1,64,128]{4,3,0,1,2:T(8,128)S(1)} collective-permute-done((f32[2,3,1,64,128]{4,3,0,1,2:T(8,128)}, f32[2,3,1,64,128]{4,3,0,1,2:T(8,128)S(1)}, u32[]{:S(2)}, u32[]{:S(2)}) %collective-permute-start.12) | collective-permute-done | bytes 196640 | tf_op jit(solution)/shard_map/ppermute | solution.py:17
  111.9 0.9 copy-done.21
  115.0 1.8 %collective-permute-start.14 = (f32[2,3,1,64,128]{4,3,0,1,2:T(8,128)S(1)}, f32[2,3,1,64,128]{4,3,0,1,2:T(8,128)S(1)}, u32[]{:S(2)}, u32[]{:S(2)}) collective-permute-start(f32[2,3,1,64,128]{4,3,0,1,2:T(8,128)S(1)} %get-tuple-element.85), channel_id=1, source_target_pairs={{2,0},{4,2},{6,4},{8,6},{10,8},{12,10},{14,12},{0,14},{3,1},{5,3},... | collective-permute-start | bytes 589832 | tf_op jit(solution)/shard_map/ppermute | solution.py:17
  118.5 3.0 %collective-permute-done.14 = f32[2,3,1,64,128]{4,3,0,1,2:T(8,128)S(1)} collective-permute-done((f32[2,3,1,64,128]{4,3,0,1,2:T(8,128)S(1)}, f32[2,3,1,64,128]{4,3,0,1,2:T(8,128)S(1)}, u32[]{:S(2)}, u32[]{:S(2)}) %collective-permute-start.14) | collective-permute-done | bytes 196640 | tf_op jit(solution)/shard_map/ppermute | solution.py:17
  121.8 0.9 copy-done.2
  123.1 0.9 copy.688
  124.1 0.8 pad_maximum_fusion.1
  (205 shorter events, 28.9 us)
Async XLA Ops:
  2.9 7.3 %collective-permute-start.1 = (f32[2,3,2,1,128]{4,3,0,1,2:T(1,128)S(1)}, f32[2,3,2,1,128]{4,3,0,1,2:T(1,128)S(1)}, u32[]{:S(2)}, u32[]{:S(2)}) collective-permute-start(f32[2,3,2,1,128]{4,3,0,1,2:T(1,128)S(1)} %slice.486), channel_id=1, source_target_pairs={{1,0},{0,1},{3,2},{2,3},{5,4},{4,5},{7,6},{6,7},{9,8},{8,9},{11,10... | collective-permute-start | bytes 18440 | tf_op jit(solution)/shard_map/ppermute | solution.py:17
  4.3 11.4 %collective-permute-start = (f32[2,3,1,64,128]{4,3,0,1,2:T(8,128)}, f32[2,3,1,64,128]{4,3,0,1,2:T(8,128)}, u32[]{:S(2)}, u32[]{:S(2)}) collective-permute-start(f32[2,3,1,64,128]{4,3,0,1,2:T(8,128)} %get-tuple-element.116), channel_id=1, source_target_pairs={{14,0},{0,2},{2,4},{4,6},{6,8},{8,10},{10,12},{12,14},{15,1},{1,3}... | collective-permute-start | bytes 589832 | tf_op jit(solution)/shard_map/ppermute | solution.py:17
  6.9 1.2 copy-start.43
  8.1 29.5 %copy-start.4 = (f32[2,64,128]{2,1,0:T(8,128)}, f32[2,64,128]{2,1,0:T(8,128)S(1)}, u32[]{:S(2)}) copy-start(f32[2,64,128]{2,1,0:T(8,128)S(1)} %get-tuple-element.67) | copy-start | bytes 196612
  8.1 41.1 %copy-start.7 = (f32[2,64,128]{2,1,0:T(8,128)}, f32[2,64,128]{2,1,0:T(8,128)S(1)}, u32[]{:S(2)}) copy-start(f32[2,64,128]{2,1,0:T(8,128)S(1)} %get-tuple-element.68) | copy-start | bytes 196612
  8.1 43.1 %copy-start.10 = (f32[2,64,128]{2,1,0:T(8,128)}, f32[2,64,128]{2,1,0:T(8,128)S(1)}, u32[]{:S(2)}) copy-start(f32[2,64,128]{2,1,0:T(8,128)S(1)} %get-tuple-element.70) | copy-start | bytes 196612
  8.1 49.1 %copy-start.13 = (f32[2,64,128]{2,1,0:T(8,128)}, f32[2,64,128]{2,1,0:T(8,128)S(1)}, u32[]{:S(2)}) copy-start(f32[2,64,128]{2,1,0:T(8,128)S(1)} %get-tuple-element.69) | copy-start | bytes 196612
  18.4 6.0 %collective-permute-start.3 = (f32[2,3,2,1,128]{4,3,0,1,2:T(1,128)}, f32[2,3,2,1,128]{4,3,0,1,2:T(1,128)}, u32[]{:S(2)}, u32[]{:S(2)}) collective-permute-start(f32[2,3,2,1,128]{4,3,0,1,2:T(1,128)} %slice.499), channel_id=1, source_target_pairs={{1,0},{0,1},{3,2},{2,3},{5,4},{4,5},{7,6},{6,7},{9,8},{8,9},{11,10... | collective-permute-start | bytes 18440 | tf_op jit(solution)/shard_map/ppermute | solution.py:17
  22.0 7.6 %collective-permute-start.2 = (f32[2,3,1,64,128]{4,3,0,2,1:T(8,128)}, f32[2,3,1,64,128]{4,3,0,2,1:T(8,128)}, u32[]{:S(2)}, u32[]{:S(2)}) collective-permute-start(f32[2,3,1,64,128]{4,3,0,2,1:T(8,128)} %get-tuple-element.120), channel_id=1, source_target_pairs={{2,0},{4,2},{6,4},{8,6},{10,8},{12,10},{14,12},{0,14},{3,1},{5,3},... | collective-permute-start | bytes 589832 | tf_op jit(solution)/shard_map/ppermute | solution.py:17
  29.6 1.5 %copy-start.40 = (f32[2,1,1,2,64,128]{5,4,0,3,2,1:T(8,128)S(1)}, f32[2,1,1,2,64,128]{5,4,0,3,2,1:T(8,128)}, u32[]{:S(2)}) copy-start(f32[2,1,1,2,64,128]{5,4,0,3,2,1:T(8,128)} %get-tuple-element.155) | copy-start | bytes 393220
  30.9 1.0 copy-start.24
  30.9 1.1 copy-start.25
  30.9 1.2 copy-start.31
  31.0 1.2 copy-start.36
  31.0 1.2 copy-start.37
  31.0 1.2 copy-start.38
  31.0 1.3 %copy-start.39 = (f32[2,1,1,2,64,128]{5,4,0,3,2,1:T(8,128)S(1)}, f32[2,1,1,2,64,128]{5,4,0,3,2,1:T(8,128)}, u32[]{:S(2)}) copy-start(f32[2,1,1,2,64,128]{5,4,0,3,2,1:T(8,128)} %get-tuple-element.44) | copy-start | bytes 393220
  32.3 1.4 %copy-start = (f32[2,2,3,2,64,128]{5,4,3,2,1,0:T(8,128)S(1)}, f32[2,2,3,2,64,128]{5,4,3,2,1,0:T(8,128)}, u32[]{:S(2)}) copy-start(f32[2,2,3,2,64,128]{5,4,3,2,1,0:T(8,128)} %param.4) | copy-start | bytes 2359300
  36.6 2.3 %collective-permute-start.5 = (f32[2,3,2,1,128]{4,3,0,2,1:T(1,128)S(1)}, f32[2,3,2,1,128]{4,3,0,2,1:T(1,128)S(1)}, u32[]{:S(2)}, u32[]{:S(2)}) collective-permute-start(f32[2,3,2,1,128]{4,3,0,2,1:T(1,128)S(1)} %slice.512), channel_id=1, source_target_pairs={{1,0},{0,1},{3,2},{2,3},{5,4},{4,5},{7,6},{6,7},{9,8},{8,9},{11,10... | collective-permute-start | bytes 18440 | tf_op jit(solution)/shard_map/ppermute | solution.py:17
  37.6 10.3 %collective-permute-start.4 = (f32[2,3,1,64,128]{4,3,0,1,2:T(8,128)}, f32[2,3,1,64,128]{4,3,0,1,2:T(8,128)}, u32[]{:S(2)}, u32[]{:S(2)}) collective-permute-start(f32[2,3,1,64,128]{4,3,0,1,2:T(8,128)} %get-tuple-element.102), channel_id=1, source_target_pairs={{14,0},{0,2},{2,4},{4,6},{6,8},{8,10},{10,12},{12,14},{15,1},{1,3}... | collective-permute-start | bytes 589832 | tf_op jit(solution)/shard_map/ppermute | solution.py:17
  49.4 6.6 %collective-permute-start.6 = (f32[2,3,1,64,128]{4,3,0,1,2:T(8,128)S(1)}, f32[2,3,1,64,128]{4,3,0,1,2:T(8,128)S(1)}, u32[]{:S(2)}, u32[]{:S(2)}) collective-permute-start(f32[2,3,1,64,128]{4,3,0,1,2:T(8,128)S(1)} %get-tuple-element.110), channel_id=1, source_target_pairs={{2,0},{4,2},{6,4},{8,6},{10,8},{12,10},{14,12},{0,14},{3,1},{5,3},... | collective-permute-start | bytes 589832 | tf_op jit(solution)/shard_map/ppermute | solution.py:17
  51.3 1.2 collective-permute-start.7
  57.5 1.0 copy-start.18
  57.5 1.1 copy-start.19
  57.6 1.2 copy-start.20
  57.6 1.3 %copy-start.32 = (f32[2,1,3,1,64,128]{5,4,0,2,3,1:T(8,128)S(1)}, f32[2,1,3,1,64,128]{5,4,0,2,3,1:T(8,128)}, u32[]{:S(2)}) copy-start(f32[2,1,3,1,64,128]{5,4,0,2,3,1:T(8,128)} %get-tuple-element.100) | copy-start | bytes 589828
  64.1 3.7 %collective-permute-start.9 = (f32[2,3,2,1,128]{4,3,0,1,2:T(1,128)}, f32[2,3,2,1,128]{4,3,0,1,2:T(1,128)S(1)}, u32[]{:S(2)}, u32[]{:S(2)}) collective-permute-start(f32[2,3,2,1,128]{4,3,0,1,2:T(1,128)} %slice.538), channel_id=1, source_target_pairs={{1,0},{0,1},{3,2},{2,3},{5,4},{4,5},{7,6},{6,7},{9,8},{8,9},{11,10... | collective-permute-start | bytes 18440 | tf_op jit(solution)/shard_map/ppermute | solution.py:17
  64.1 10.3 %collective-permute-start.8 = (f32[2,3,1,64,128]{4,3,0,1,2:T(8,128)}, f32[2,3,1,64,128]{4,3,0,1,2:T(8,128)}, u32[]{:S(2)}, u32[]{:S(2)}) collective-permute-start(f32[2,3,1,64,128]{4,3,0,1,2:T(8,128)} %get-tuple-element.90), channel_id=1, source_target_pairs={{14,0},{0,2},{2,4},{4,6},{6,8},{8,10},{10,12},{12,14},{15,1},{1,3}... | collective-permute-start | bytes 589832 | tf_op jit(solution)/shard_map/ppermute | solution.py:17
  74.4 3.0 %copy-start.3 = (f32[2,3,2,64,1]{4,3,0,1,2:T(8,128)S(1)}, f32[2,3,2,64,1]{4,3,0,1,2:T(8,128)}, u32[]{:S(2)}) copy-start(f32[2,3,2,64,1]{4,3,0,1,2:T(8,128)} %slice.543) | copy-start | bytes 9220
  74.4 3.0 %copy-start.29 = (f32[2,3,2,64,127]{4,3,0,1,2:T(8,128)S(1)}, f32[2,3,2,64,127]{4,3,0,1,2:T(8,128)}, u32[]{:S(2)}) copy-start(f32[2,3,2,64,127]{4,3,0,1,2:T(8,128)} %get-tuple-element.94) | copy-start | bytes 1170436
  74.4 3.0 %copy-start.30 = (f32[2,3,2,63,128]{4,3,0,1,2:T(8,128)S(1)}, f32[2,3,2,63,128]{4,3,0,1,2:T(8,128)}, u32[]{:S(2)}) copy-start(f32[2,3,2,63,128]{4,3,0,1,2:T(8,128)} %get-tuple-element.92) | copy-start | bytes 1161220
  74.4 3.0 %copy-start.35 = (f32[2,3,1,64,128]{4,3,0,1,2:T(8,128)S(1)}, f32[2,3,1,64,128]{4,3,0,1,2:T(8,128)}, u32[]{:S(2)}) copy-start(f32[2,3,1,64,128]{4,3,0,1,2:T(8,128)} %get-tuple-element.89) | copy-start | bytes 589828
  77.4 1.2 copy-start.11
  83.0 6.1 %collective-permute-start.11 = (f32[2,3,2,1,128]{4,3,0,2,1:T(1,128)}, f32[2,3,2,1,128]{4,3,0,2,1:T(1,128)S(1)}, u32[]{:S(2)}, u32[]{:S(2)}) collective-permute-start(f32[2,3,2,1,128]{4,3,0,2,1:T(1,128)} %slice.551), channel_id=1, source_target_pairs={{1,0},{0,1},{3,2},{2,3},{5,4},{4,5},{7,6},{6,7},{9,8},{8,9},{11,10... | collective-permute-start | bytes 18440 | tf_op jit(solution)/shard_map/ppermute | solution.py:17
  85.3 7.6 %collective-permute-start.10 = (f32[2,3,1,64,128]{4,3,0,2,1:T(8,128)}, f32[2,3,1,64,128]{4,3,0,2,1:T(8,128)}, u32[]{:S(2)}, u32[]{:S(2)}) collective-permute-start(f32[2,3,1,64,128]{4,3,0,2,1:T(8,128)} %get-tuple-element.96), channel_id=1, source_target_pairs={{2,0},{4,2},{6,4},{8,6},{10,8},{12,10},{14,12},{0,14},{3,1},{5,3},... | collective-permute-start | bytes 589832 | tf_op jit(solution)/shard_map/ppermute | solution.py:17
  88.0 4.9 %copy-start.16 = (f32[2,1,3,2,64,128]{5,4,0,2,3,1:T(8,128)S(1)}, f32[2,1,3,2,64,128]{5,4,0,2,3,1:T(8,128)}, u32[]{:S(2)}) copy-start(f32[2,1,3,2,64,128]{5,4,0,2,3,1:T(8,128)} %get-tuple-element.53) | copy-start | bytes 1179652
  88.2 4.7 %copy-start.17 = (f32[2,1,3,2,64,128]{5,4,0,2,3,1:T(8,128)S(1)}, f32[2,1,3,2,64,128]{5,4,0,2,3,1:T(8,128)}, u32[]{:S(2)}) copy-start(f32[2,1,3,2,64,128]{5,4,0,2,3,1:T(8,128)} %get-tuple-element.54) | copy-start | bytes 1179652
  100.3 11.5 %collective-permute-start.13 = (f32[2,3,2,1,128]{4,3,0,1,2:T(1,128)S(1)}, f32[2,3,2,1,128]{4,3,0,1,2:T(1,128)S(1)}, u32[]{:S(2)}, u32[]{:S(2)}) collective-permute-start(f32[2,3,2,1,128]{4,3,0,1,2:T(1,128)S(1)} %slice.564), channel_id=1, source_target_pairs={{1,0},{0,1},{3,2},{2,3},{5,4},{4,5},{7,6},{6,7},{9,8},{8,9},{11,10... | collective-permute-start | bytes 18440 | tf_op jit(solution)/shard_map/ppermute | solution.py:17
  101.5 10.2 %copy-start.34 = (f32[2,1,3,1,64,128]{5,4,0,2,3,1:T(8,128)S(1)}, f32[2,1,3,1,64,128]{5,4,0,2,3,1:T(8,128)}, u32[]{:S(2)}) copy-start(f32[2,1,3,1,64,128]{5,4,0,2,3,1:T(8,128)} %get-tuple-element.75) | copy-start | bytes 589828
  101.5 10.2 %collective-permute-start.12 = (f32[2,3,1,64,128]{4,3,0,1,2:T(8,128)}, f32[2,3,1,64,128]{4,3,0,1,2:T(8,128)S(1)}, u32[]{:S(2)}, u32[]{:S(2)}) collective-permute-start(f32[2,3,1,64,128]{4,3,0,1,2:T(8,128)} %get-tuple-element.77), channel_id=1, source_target_pairs={{14,0},{0,2},{2,4},{4,6},{6,8},{8,10},{10,12},{12,14},{15,1},{1,3}... | collective-permute-start | bytes 589832 | tf_op jit(solution)/shard_map/ppermute | solution.py:17
  111.7 1.0 copy-start.21
  111.7 1.1 copy-start.22
  111.7 1.2 copy-start.33
  115.0 6.6 %collective-permute-start.14 = (f32[2,3,1,64,128]{4,3,0,1,2:T(8,128)S(1)}, f32[2,3,1,64,128]{4,3,0,1,2:T(8,128)S(1)}, u32[]{:S(2)}, u32[]{:S(2)}) collective-permute-start(f32[2,3,1,64,128]{4,3,0,1,2:T(8,128)S(1)} %get-tuple-element.85), channel_id=1, source_target_pairs={{2,0},{4,2},{6,4},{8,6},{10,8},{12,10},{14,12},{0,14},{3,1},{5,3},... | collective-permute-start | bytes 589832 | tf_op jit(solution)/shard_map/ppermute | solution.py:17
  116.8 1.1 copy-start.26
  116.8 1.2 copy-start.27
  116.9 1.6 %collective-permute-start.15 = (f32[2,3,2,1,128]{4,3,2,0,1:T(1,128)S(1)}, f32[2,3,2,1,128]{4,3,2,0,1:T(1,128)S(1)}, u32[]{:S(2)}, u32[]{:S(2)}) collective-permute-start(f32[2,3,2,1,128]{4,3,2,0,1:T(1,128)S(1)} %slice.577), channel_id=1, source_target_pairs={{1,0},{0,1},{3,2},{2,3},{5,4},{4,5},{7,6},{6,7},{9,8},{8,9},{11,10... | collective-permute-start | bytes 18440 | tf_op jit(solution)/shard_map/ppermute | solution.py:17
  121.6 1.1 copy-start.2
  (12 other events, 11.0 us)
where the time goes:
time: 126 us; the launch traced here: 125 us
  waiting for transfers between devices  46.8 us (37%)
  local copies, waits for them, and re-layouts  35.1 us (28%)
  other arithmetic  31.2 us (25%)
  starting transfers between devices  10.4 us (8%)
  between operations  1.5 us (1%)
    ppermute x16, waiting for transfers between devices, passed_along(): return lax.ppermute(block, axis, route)  46.8 us
    another operation x27, other arithmetic, bond_force(): return stiff_trans * diff + jnp.stack(parts, axis=1)  10.4 us
    ppermute x16, starting transfers between devices, passed_along(): return lax.ppermute(block, axis, route)  10.4 us
    unnamed x89, local copies, waits for them, and re-layouts  9.57 us
    concatenate x8, local copies, waits for them, and re-layouts, operate_sending(): lower = jnp.roll(upper_b, 1, axis=4)  7.61 us
    mul x6, other arithmetic, bond_force(): return stiff_trans * diff + jnp.stack(parts, axis=1)  6.23 us
    add x5, other arithmetic, operate_sending(): force_a = force_a + term  5.51 us
    concatenate x4, local copies, waits for them, and re-layouts, operate_sending(): lower = jnp.concatenate([plane, upper_b[:, :, :-1]], axis=2)  3.45 us
  transfers between devices with their start and end apart: 16, of which 9 were waited for; matrix products, arithmetic and copies ran while one was open for 17% of the time, Pallas kernels for 0%

commit v1 on v0

v1 whole, which is shorter than its diff:
```python
import functools

import jax
import jax.numpy as jnp
from jax import lax
from jax.experimental import pallas as pl
from jax.experimental.pallas import tpu as pltpu
from jax.sharding import PartitionSpec as P

STEPS = 4
SIGNS = ((1, 1, 1), (1, -1, -1), (-1, 1, -1), (-1, -1, 1))
MESH = pl.DeviceIdType.MESH


def signed(x, sign, y):
    return x + y if sign > 0 else x - y


def add_bond(total, upper, lower, trans, extra, which):
    signs = SIGNS[which]
    diff = [upper[c] - lower[c] for c in range(3)]
    along = signed(signed(diff[0], signs[0] * signs[1], diff[1]), signs[0] * signs[2], diff[2])
    along = extra * along
    for c in range(3):
        part = trans * diff[c]
        part = signed(part, signs[c] * signs[0], along)
        total[c] = part if total[c] is None else total[c] + part
    return total


def kernel(
    ring, start_hbm, mass_hbm, long_hbm, trans_hbm, last_hbm, dens_hbm,
    start, mass, long, trans, scale, tran_a, extr_a, tran_b, extr_b,
    u, t, dens, halo, row_out, row_in, bond_in, rowbond_out, rowbond_in,
    load_sem, save_sem, x_send, x_recv, row_send, row_recv, bond_send, bond_recv, rowbond_send, rowbond_recv,
):
    vecs, _, _, planes, rows, lanes = start.shape
    me = lax.axis_index("gx")
    core = lax.axis_index("yz")
    right, left = lax.rem(me + 1, ring), lax.rem(me + ring - 1, ring)
    other = 1 - core

    loads = [
        pltpu.make_async_copy(src, dst, load_sem.at[i])
        for i, (src, dst) in enumerate(
            ((mass_hbm, mass), (start_hbm, start), (long_hbm, long), (trans_hbm, trans))
        )
    ]
    for load in loads:
        load.start()

    barrier = pltpu.get_barrier_semaphore()
    for target in ({"gx": left}, {"gx": right}, {"yz": other}):
        pl.semaphore_signal(barrier, inc=1, device_id=target, device_id_type=MESH)

    row_index = lax.broadcasted_iota(jnp.int32, (rows, lanes), 0)
    first_row, last_row = row_index == 0, row_index == rows - 1

    def x_copy(n, v, side):
        src = u.at[n, v, 1, planes - 1] if side == 0 else u.at[n, v, 0, 0]
        return pltpu.make_async_remote_copy(
            src_ref=src, dst_ref=halo.at[n, v, side],
            send_sem=x_send.at[n, v, side], recv_sem=x_recv.at[n, v, side],
            device_id={"gx": right if side == 0 else left}, device_id_type=MESH,
        )

    def row_copy(n, v):
        return pltpu.make_async_remote_copy(
            src_ref=row_out.at[n, v], dst_ref=row_in.at[n, v],
            send_sem=row_send.at[n, v], recv_sem=row_recv.at[n, v],
            device_id={"yz": other}, device_id_type=MESH,
        )

    def bond_copy(i):
        src = (long_hbm, trans_hbm)[i]
        return pltpu.make_async_remote_copy(
            src_ref=src.at[1, 0], dst_ref=bond_in.at[i],
            send_sem=bond_send.at[i], recv_sem=bond_recv.at[i],
            device_id={"gx": left}, device_id_type=MESH,
        )

    rowbond_copy = pltpu.make_async_remote_copy(
        src_ref=rowbond_out, dst_ref=rowbond_in, send_sem=rowbond_send, recv_sem=rowbond_recv,
        device_id={"yz": other}, device_id_type=MESH,
    )

    def put_rows(n, v, sub, plane):
        edge = 0 if sub == 0 else rows - 1
        for c in range(3):
            row_out[n, v, sub, plane * 3 + c] = u[n, v, sub, plane, c, edge]

    def first_u(v, sub, plane):
        for c in range(3):
            u[0, v, sub, plane, c] = scale[sub, plane] * start[v, sub, c, plane]
        put_rows(0, v, sub, plane)

    loads[0].wait()
    scale[...] = lax.rsqrt(mass[...])
    loads[1].wait()
    first_u(0, 1, planes - 1)
    first_u(0, 0, 0)
    pl.semaphore_wait(barrier, 3)
    x_copy(0, 0, 0).start()
    x_copy(0, 0, 1).start()
    for i in range(2):
        bond_copy(i).start()
    first_u(1, 1, planes - 1)
    first_u(1, 0, 0)
    for v in range(1, vecs):
        x_copy(0, v, 0).start()
        x_copy(0, v, 1).start()
    for v in range(vecs):
        for plane in range(planes - 1):
            first_u(v, 1, plane)
            first_u(v, 0, plane + 1)
        row_copy(0, v).start()

    loads[2].wait()
    loads[3].wait()

    def scaled_extra(stiff_long, stiff_trans):
        return (stiff_long - stiff_trans) * (1.0 / 24.0)

    for plane in range(planes):
        for b in range(4):
            tran_a[b, plane] = trans[b, plane] * 0.125
            extr_a[b, plane] = scaled_extra(long[b, plane], trans[b, plane])
        rowbond_out[plane] = tran_a[2, plane, 0]
        rowbond_out[planes + plane] = extr_a[2, plane, 0]
    rowbond_copy.start()
    for plane in range(planes):
        for i, (coef_a, coef_b) in enumerate(((tran_a, tran_b), (extr_a, extr_b))):
            coef_b[1, plane] = pltpu.roll(coef_a[3, plane], lanes - 1, 1)
    rowbond_copy.wait_recv()
    for plane in range(planes):
        for i, (coef_a, coef_b) in enumerate(((tran_a, tran_b), (extr_a, extr_b))):
            turned = pltpu.roll(coef_a[2, plane], rows - 1, 0)
            edge = rowbond_in[i * planes + plane].reshape(1, lanes)
            coef_b[0, plane] = jnp.where(last_row, edge, turned)

    def update(n, v, sub, plane):
        own = [u[n, v, sub, plane, c] for c in range(3)]
        near = [u[n, v, 1 - sub, plane, c] for c in range(3)]
        if sub == 0:
            beside = [halo[n, v, 0, c] if plane == 0 else u[n, v, 1, plane - 1, c] for c in range(3)]
        else:
            beside = [halo[n, v, 1, c] if plane == planes - 1 else u[n, v, 0, plane + 1, c] for c in range(3)]
        edges = [row_in[n, v, 1 - sub, plane * 3 + c].reshape(1, lanes) for c in range(3)]
        shift, at_edge = (1, first_row) if sub == 0 else (rows - 1, last_row)
        along_y = [jnp.where(at_edge, edges[c], pltpu.roll(near[c], shift, 0)) for c in range(3)]
        along_z = [pltpu.roll(near[c], 1 if sub == 0 else lanes - 1, 1) for c in range(3)]
        total = [None] * 3
        for b, far in enumerate((near, beside, along_y, along_z)):
            if sub == 0 or b == 0:
                coef = tran_a[b, plane], extr_a[b, plane]
            elif b == 1 and plane == planes - 1:
                coef = bond_in[2], bond_in[3]
            elif b == 1:
                coef = tran_a[1, plane + 1], extr_a[1, plane + 1]
            else:
                coef = tran_b[b - 2, plane], extr_b[b - 2, plane]
            total = add_bond(total, own, far, *coef, b)
        own_scale = scale[sub, plane]
        gain = own_scale if n == 0 else own_scale + own_scale
        moment = None
        for c in range(3):
            first = start[v, sub, c, plane]
            now = first if n == 0 else t[n - 1, v, sub, c, plane]
            new = gain * total[c]
            if n == 0:
                new = new - now
            else:
                before = first if n == 1 else t[n - 2, v, sub, c, plane]
                new = new - (now + now) - before
            t[n, v, sub, c, plane] = new
            if n < STEPS - 1:
                u[n + 1, v, sub, plane, c] = own_scale * new
            moment = first * new if moment is None else moment + first * new
        if v == 0:
            dens[n, sub, plane] = moment
        else:
            dens[n, sub, plane] += moment
        if n < STEPS - 1:
            put_rows(n + 1, v, sub, plane)

    saves = []
    for n in range(STEPS):
        for v in range(vecs):
            row_copy(n, v).wait_recv()
            for plane in range(planes - 1):
                update(n, v, 0, plane + 1)
                update(n, v, 1, plane)
            x_copy(n, v, 0).wait_recv()
            update(n, v, 0, 0)
            if n < STEPS - 1:
                x_copy(n + 1, v, 1).start()
            x_copy(n, v, 1).wait_recv()
            if n == 0 and v == 0:
                for i in range(2):
                    bond_copy(i).wait_recv()
                bond_in[2] = bond_in[1] * 0.125
                bond_in[3] = scaled_extra(bond_in[0], bond_in[1])
            update(n, v, 1, planes - 1)
            if n < STEPS - 1:
                x_copy(n + 1, v, 0).start()
                row_copy(n + 1, v).start()
            else:
                saves.append(pltpu.make_async_copy(t.at[n, v], last_hbm.at[v], save_sem.at[STEPS + v]))
                saves[-1].start()
        saves.append(pltpu.make_async_copy(dens.at[n], dens_hbm.at[n], save_sem.at[n]))
        saves[-1].start()

    for n in range(STEPS):
        for v in range(vecs):
            row_copy(n, v).wait_send()
            for side in range(2):
                x_copy(n, v, side).wait_send()
    for i in range(2):
        bond_copy(i).wait_send()
    rowbond_copy.wait_send()
    for save in saves:
        save.wait()


def on_device(ring, start, masses, bond_long, bond_trans):
    vecs, _, _, planes, rows, lanes = start.shape
    f32 = jnp.float32
    plane = (rows, lanes)
    vmem = lambda *shape: pltpu.VMEM(shape, f32)
    dma = lambda *shape: pltpu.SemaphoreType.DMA(shape)
    padded = -(-3 * planes // 8) * 8
    padded_bonds = -(-2 * planes // 8) * 8
    return pl.pallas_call(
        functools.partial(kernel, ring),
        out_shape=(
            jax.ShapeDtypeStruct(start.shape, f32),
            jax.ShapeDtypeStruct((STEPS, 2, planes, rows, lanes), f32),
        ),
        in_specs=[pl.BlockSpec(memory_space=pl.ANY)] * 4,
        out_specs=(pl.BlockSpec(memory_space=pl.ANY),) * 2,
        scratch_shapes=[
            vmem(*start.shape), vmem(*masses.shape), vmem(*bond_long.shape), vmem(*bond_trans.shape),
            vmem(*masses.shape),
            vmem(4, planes, *plane), vmem(4, planes, *plane), vmem(2, planes, *plane), vmem(2, planes, *plane),
            vmem(STEPS, vecs, 2, planes, 3, *plane),
            vmem(STEPS, *start.shape),
            vmem(STEPS, 2, planes, *plane),
            vmem(STEPS, vecs, 2, 3, *plane),
            vmem(STEPS, vecs, 2, padded, lanes), vmem(STEPS, vecs, 2, padded, lanes),
            vmem(4, *plane),
            vmem(padded_bonds, lanes), vmem(padded_bonds, lanes),
            dma(4), dma(STEPS + vecs),
            dma(STEPS, vecs, 2), dma(STEPS, vecs, 2), dma(STEPS, vecs), dma(STEPS, vecs),
            dma(2), dma(2), pltpu.SemaphoreType.DMA, pltpu.SemaphoreType.DMA,
        ],
        compiler_params=pltpu.CompilerParams(
            collective_id=0, has_side_effects=True, vmem_limit_bytes=32 * 1024 * 1024
        ),
        name="chebyshev",
    )(start, masses, bond_long, bond_trans)


def solution(mesh):
    in_specs = (
        P(None, None, None, ("grp", "gx"), "yz", None),
        P(None, ("grp", "gx"), "yz", None),
        P(None, ("grp", "gx"), "yz", None),
        P(None, ("grp", "gx"), "yz", None),
    )
    out_specs = (
        P(None, None, None, ("grp", "gx"), "yz", None),
        P(None, None, ("grp", "gx"), "yz", None),
    )
    return jax.shard_map(
        functools.partial(on_device, mesh.shape["gx"]),
        mesh=mesh, in_specs=in_specs, out_specs=out_specs, check_vma=False,
    )
```

time: 126 us -> 51.4 us (0.41)
  waiting for transfers between devices: 46.8 us -> 0 us
  Pallas kernels: 0 us -> 44.9 us
  other arithmetic: 31.2 us -> 0 us
  local copies, waits for them, and re-layouts: 35.1 us -> 5.6 us
  starting transfers between devices: 10.4 us -> 0 us
    ppermute x16 -> x0, waiting for transfers between devices: 46.8 us -> none  [passed_along(): return lax.ppermute(block, axis, route)]
    pallas_call x0 -> x1, Pallas kernels: none -> 44.9 us  [on_device(): pl.pallas_call(functools.partial(kernel, ring), out_shape=(jax.ShapeDtype...]
    concatenate x33 -> x0, local copies, waits for them, and re-layouts: 19.1 us -> none  [the longest x8 7.61 us: operate_sending(): lower = jnp.roll(upper_b, 1, axis=4)]
    another operation x28 -> x0, other arithmetic: 11.3 us -> none  [the longest x27 10.4 us: bond_force(): return stiff_trans * diff + jnp.stack(parts, axis=1)]
    ppermute x16 -> x0, starting transfers between devices: 10.4 us -> none  [passed_along(): return lax.ppermute(block, axis, route)]
    mul x14 -> x0, other arithmetic: 7.78 us -> none  [the longest x6 6.23 us: bond_force(): return stiff_trans * diff + jnp.stack(parts, axis=1)]
    add x17 -> x0, other arithmetic: 6.11 us -> none  [the longest x5 5.51 us: operate_sending(): force_a = force_a + term]
    slice x20 -> x0, local copies, waits for them, and re-layouts: 5.33 us -> none  [the longest x8 3.05 us: operate_sending(): lower = jnp.roll(upper_b, 1, axis=4)]
  transfers between devices with their start and end apart: 16 -> 0, of which waited for: 9 -> 0; matrix products, arithmetic and copies ran while one was open for 17% -> 0% of each run, Pallas kernels for 0% -> 0%
where the time goes in v1:
time: 51.4 us; the launch traced here: 51.1 us
  Pallas kernels  44.9 us (87%)
  local copies, waits for them, and re-layouts  5.6 us (11%)
  between operations  0.65 us (1%)
    pallas_call x1, Pallas kernels, on_device(): pl.pallas_call(functools.partial(kernel, ring), out_shape=(jax.ShapeDtype...  44.9 us
    unnamed x10, local copies, waits for them, and re-layouts  5.6 us

profile of v1, /device:TPU:0, one launch (start us, length us, event | category | flops | bytes accessed | tf_op | source)
XLA Modules:
  0.0 51.1 jit_solution(11177994642840774724)
XLA Ops:
  0.6 0.0 copy-start
  0.6 1.1 %copy-done = f32[2,2,3,2,64,128]{5,4,3,2,1,0:T(8,128)S(1)} copy-done((f32[2,2,3,2,64,128]{5,4,3,2,1,0:T(8,128)S(1)}, f32[2,2,3,2,64,128]{5,4,3,2,1,0:T(8,128)}, u32[]{:S(2)}) %copy-start) | copy-done | bytes 786456
  1.8 0.0 copy-start.1
  1.8 0.9 %copy-done.1 = f32[4,2,64,128]{3,2,1,0:T(8,128)S(1)} copy-done((f32[4,2,64,128]{3,2,1,0:T(8,128)S(1)}, f32[4,2,64,128]{3,2,1,0:T(8,128)}, u32[]{:S(2)}) %copy-start.1) | copy-done | bytes 262168
  2.7 0.0 copy-start.2
  2.7 0.9 %copy-done.2 = f32[4,2,64,128]{3,2,1,0:T(8,128)S(1)} copy-done((f32[4,2,64,128]{3,2,1,0:T(8,128)S(1)}, f32[4,2,64,128]{3,2,1,0:T(8,128)}, u32[]{:S(2)}) %copy-start.2) | copy-done | bytes 262168
  3.7 0.0 copy-start.3
  3.7 0.9 %copy-done.3 = f32[2,2,64,128]{3,2,1,0:T(8,128)S(1)} copy-done((f32[2,2,64,128]{3,2,1,0:T(8,128)S(1)}, f32[2,2,64,128]{3,2,1,0:T(8,128)}, u32[]{:S(2)}) %copy-start.3) | copy-done | bytes 131096
  4.6 44.9 %chebyshev.1 = (f32[2,2,3,2,64,128]{5,4,3,2,1,0:T(8,128)S(1)}, f32[4,2,2,64,128]{4,3,2,1,0:T(8,128)S(1)}) custom-call(f32[2,2,3,2,64,128]{5,4,3,2,1,0:T(8,128)S(1)} %copy-done, f32[2,2,64,128]{3,2,1,0:T(8,128)S(1)} %copy-done.3, f32[4,2,64,128]{3,2,1,0:T(8,128)S(1)} %copy-done.1, f32[4,2,64,128]{3,2,1,0:T(8,128)S(1)} %copy-done.2), custom_call_target="tpu_custom_call" | custom-call | tf_op jit(solution)/shard_map/chebyshev/pallas_call | solution.py:233
  49.5 0.9 %copy.8 = f32[2,2,3,2,64,128]{5,4,3,2,1,0:T(8,128)} copy(f32[2,2,3,2,64,128]{5,4,3,2,1,0:T(8,128)S(1)} %get-tuple-element.4) | data formatting | bytes 1572864
  50.3 0.8 %copy.9 = f32[4,2,2,64,128]{4,3,2,1,0:T(8,128)} copy(f32[4,2,2,64,128]{4,3,2,1,0:T(8,128)S(1)} %get-tuple-element.5) | data formatting | bytes 1048576
Async XLA Ops:
  0.6 1.1 %copy-start = (f32[2,2,3,2,64,128]{5,4,3,2,1,0:T(8,128)S(1)}, f32[2,2,3,2,64,128]{5,4,3,2,1,0:T(8,128)}, u32[]{:S(2)}) copy-start(f32[2,2,3,2,64,128]{5,4,3,2,1,0:T(8,128)} %start_hbm.1) | copy-start | bytes 2359300
  1.8 0.9 %copy-start.1 = (f32[4,2,64,128]{3,2,1,0:T(8,128)S(1)}, f32[4,2,64,128]{3,2,1,0:T(8,128)}, u32[]{:S(2)}) copy-start(f32[4,2,64,128]{3,2,1,0:T(8,128)} %long_hbm.1) | copy-start | bytes 786436
  2.7 0.9 %copy-start.2 = (f32[4,2,64,128]{3,2,1,0:T(8,128)S(1)}, f32[4,2,64,128]{3,2,1,0:T(8,128)}, u32[]{:S(2)}) copy-start(f32[4,2,64,128]{3,2,1,0:T(8,128)} %trans_hbm.1) | copy-start | bytes 786436
  3.7 0.9 %copy-start.3 = (f32[2,2,64,128]{3,2,1,0:T(8,128)S(1)}, f32[2,2,64,128]{3,2,1,0:T(8,128)}, u32[]{:S(2)}) copy-start(f32[2,2,64,128]{3,2,1,0:T(8,128)} %mass_hbm.1) | copy-start | bytes 393220

commit v2 on v1

--- a/solution.py
+++ b/solution.py
@@ -29,10 +29,10 @@
 
 
 def kernel(
-    ring, start_hbm, mass_hbm, long_hbm, trans_hbm, last_hbm, dens_hbm,
+    ring, start_hbm, mass_hbm, long_hbm, trans_hbm, last, dens,
     start, mass, long, trans, scale, tran_a, extr_a, tran_b, extr_b,
-    u, t, dens, halo, row_out, row_in, bond_in, rowbond_out, rowbond_in,
-    load_sem, save_sem, x_send, x_recv, row_send, row_recv, bond_send, bond_recv, rowbond_send, rowbond_recv,
+    u, t, halo, row_out, row_in, bond_in, rowbond_out, rowbond_in,
+    load_sem, x_send, x_recv, row_send, row_recv, bond_send, bond_recv, rowbond_send, rowbond_recv,
 ):
     vecs, _, _, planes, rows, lanes = start.shape
     me = lax.axis_index("gx")
@@ -172,8 +172,10 @@
             else:
                 before = first if n == 1 else t[n - 2, v, sub, c, plane]
                 new = new - (now + now) - before
-            t[n, v, sub, c, plane] = new
-            if n < STEPS - 1:
+            if n == STEPS - 1:
+                last[v, sub, c, plane] = new
+            else:
+                t[n, v, sub, c, plane] = new
                 u[n + 1, v, sub, plane, c] = own_scale * new
             moment = first * new if moment is None else moment + first * new
         if v == 0:
@@ -183,7 +185,6 @@
         if n < STEPS - 1:
             put_rows(n + 1, v, sub, plane)
 
-    saves = []
     for n in range(STEPS):
         for v in range(vecs):
             row_copy(n, v).wait_recv()
@@ -204,11 +205,6 @@
             if n < STEPS - 1:
                 x_copy(n + 1, v, 0).start()
                 row_copy(n + 1, v).start()
-            else:
-                saves.append(pltpu.make_async_copy(t.at[n, v], last_hbm.at[v], save_sem.at[STEPS + v]))
-                saves[-1].start()
-        saves.append(pltpu.make_async_copy(dens.at[n], dens_hbm.at[n], save_sem.at[n]))
-        saves[-1].start()
 
     for n in range(STEPS):
         for v in range(vecs):
@@ -218,8 +214,6 @@
     for i in range(2):
         bond_copy(i).wait_send()
     rowbond_copy.wait_send()
-    for save in saves:
-        save.wait()
 
 
 def on_device(ring, start, masses, bond_long, bond_trans):
@@ -236,20 +230,19 @@
             jax.ShapeDtypeStruct(start.shape, f32),
             jax.ShapeDtypeStruct((STEPS, 2, planes, rows, lanes), f32),
         ),
-        in_specs=[pl.BlockSpec(memory_space=pl.ANY)] * 4,
-        out_specs=(pl.BlockSpec(memory_space=pl.ANY),) * 2,
+        in_specs=[pl.BlockSpec(memory_space=pltpu.HBM)] * 4,
+        out_specs=(pl.BlockSpec(memory_space=pltpu.VMEM),) * 2,
         scratch_shapes=[
             vmem(*start.shape), vmem(*masses.shape), vmem(*bond_long.shape), vmem(*bond_trans.shape),
             vmem(*masses.shape),
             vmem(4, planes, *plane), vmem(4, planes, *plane), vmem(2, planes, *plane), vmem(2, planes, *plane),
             vmem(STEPS, vecs, 2, planes, 3, *plane),
-            vmem(STEPS, *start.shape),
-            vmem(STEPS, 2, planes, *plane),
+            vmem(STEPS - 1, *start.shape),
             vmem(STEPS, vecs, 2, 3, *plane),
             vmem(STEPS, vecs, 2, padded, lanes), vmem(STEPS, vecs, 2, padded, lanes),
             vmem(4, *plane),
             vmem(padded_bonds, lanes), vmem(padded_bonds, lanes),
-            dma(4), dma(STEPS + vecs),
+            dma(4),
             dma(STEPS, vecs, 2), dma(STEPS, vecs, 2), dma(STEPS, vecs), dma(STEPS, vecs),
             dma(2), dma(2), pltpu.SemaphoreType.DMA, pltpu.SemaphoreType.DMA,
         ],
@@ -257,7 +250,7 @@
             collective_id=0, has_side_effects=True, vmem_limit_bytes=32 * 1024 * 1024
         ),
         name="chebyshev",
-    )(start, masses, bond_long, bond_trans)
+    )(*(pltpu.with_memory_space_constraint(x, pltpu.HBM) for x in (start, masses, bond_long, bond_trans)))
 
 
 def solution(mesh):

time: 51.4 us -> 46.7 us (0.909)
  local copies, waits for them, and re-layouts: 5.6 us -> 1.67 us
  Pallas kernels: 44.9 us -> 44.3 us
    unnamed x10 -> x2, local copies, waits for them, and re-layouts: 5.6 us -> 1.67 us
    pallas_call x1, Pallas kernels: 44.9 us -> 44.3 us  [on_device(): pl.pallas_call(functools.partial(kernel, ring), out_shape=(jax.ShapeDtype...]
where the time goes in v2:
time: 46.7 us; the launch traced here: 46.6 us
  Pallas kernels  44.3 us (95%)
  local copies, waits for them, and re-layouts  1.67 us (4%)
  between operations  0.64 us (1%)
    pallas_call x1, Pallas kernels, on_device(): pl.pallas_call(functools.partial(kernel, ring), out_shape=(jax.ShapeDtype...  44.3 us
    unnamed x2, local copies, waits for them, and re-layouts  1.67 us

profile of v2, /device:TPU:0, one launch (start us, length us, event | category | flops | bytes accessed | tf_op | source)
XLA Modules:
  0.0 46.6 jit_solution(10799859428935324380)
XLA Ops:
  0.6 44.3 %chebyshev.1 = (f32[2,2,3,2,64,128]{5,4,3,2,1,0:T(8,128)S(1)}, f32[4,2,2,64,128]{4,3,2,1,0:T(8,128)S(1)}) custom-call(f32[2,2,3,2,64,128]{5,4,3,2,1,0:T(8,128)} %start_hbm.1, f32[2,2,64,128]{3,2,1,0:T(8,128)} %mass_hbm.1, f32[4,2,64,128]{3,2,1,0:T(8,128)} %long_hbm.1, f32[4,2,64,128]{3,2,1,0:T(8,128)} %trans_hbm.1), custom_call_target="tpu_custom_call" | custom-call | tf_op jit(solution)/shard_map/chebyshev/pallas_call | solution.py:227
  44.9 0.9 %copy.8 = f32[2,2,3,2,64,128]{5,4,3,2,1,0:T(8,128)} copy(f32[2,2,3,2,64,128]{5,4,3,2,1,0:T(8,128)S(1)} %get-tuple-element.4) | data formatting | bytes 1572864
  45.8 0.8 %copy.9 = f32[4,2,2,64,128]{4,3,2,1,0:T(8,128)} copy(f32[4,2,2,64,128]{4,3,2,1,0:T(8,128)S(1)} %get-tuple-element.5) | data formatting | bytes 1048576

commit v3 on v2

--- a/solution.py
+++ b/solution.py
@@ -46,7 +46,7 @@
             ((mass_hbm, mass), (start_hbm, start), (long_hbm, long), (trans_hbm, trans))
         )
     ]
-    for load in loads:
+    for load in loads[:2]:
         load.start()
 
     barrier = pltpu.get_barrier_semaphore()
@@ -94,16 +94,18 @@
             u[0, v, sub, plane, c] = scale[sub, plane] * start[v, sub, c, plane]
         put_rows(0, v, sub, plane)
 
+    pl.semaphore_wait(barrier, 3)
+    for i in range(2):
+        bond_copy(i).start()
+    for load in loads[2:]:
+        load.start()
     loads[0].wait()
     scale[...] = lax.rsqrt(mass[...])
     loads[1].wait()
     first_u(0, 1, planes - 1)
+    x_copy(0, 0, 0).start()
     first_u(0, 0, 0)
-    pl.semaphore_wait(barrier, 3)
-    x_copy(0, 0, 0).start()
     x_copy(0, 0, 1).start()
-    for i in range(2):
-        bond_copy(i).start()
     first_u(1, 1, planes - 1)
     first_u(1, 0, 0)
     for v in range(1, vecs):
@@ -216,6 +218,26 @@
     rowbond_copy.wait_send()
 
 
+def flush_kernel(last_in, dens_in, last_out, dens_out, sem):
+    pairs = [(src.at[i], dst.at[i]) for src, dst in ((last_in, last_out), (dens_in, dens_out)) for i in range(src.shape[0])]
+    copies = [pltpu.make_async_copy(src, dst, sem.at[i]) for i, (src, dst) in enumerate(pairs)]
+    for copy in copies:
+        copy.start()
+    for copy in copies:
+        copy.wait()
+
+
+def flush(last, dens):
+    return pl.pallas_call(
+        flush_kernel,
+        out_shape=tuple(jax.ShapeDtypeStruct(x.shape, x.dtype) for x in (last, dens)),
+        in_specs=[pl.BlockSpec(memory_space=pl.ANY)] * 2,
+        out_specs=(pl.BlockSpec(memory_space=pl.ANY),) * 2,
+        scratch_shapes=[pltpu.SemaphoreType.DMA((last.shape[0] + dens.shape[0],))],
+        name="flush",
+    )(*(pltpu.with_memory_space_constraint(x, pltpu.VMEM) for x in (last, dens)))
+
+
 def on_device(ring, start, masses, bond_long, bond_trans):
     vecs, _, _, planes, rows, lanes = start.shape
     f32 = jnp.float32
@@ -224,7 +246,7 @@
     dma = lambda *shape: pltpu.SemaphoreType.DMA(shape)
     padded = -(-3 * planes // 8) * 8
     padded_bonds = -(-2 * planes // 8) * 8
-    return pl.pallas_call(
+    last, dens = pl.pallas_call(
         functools.partial(kernel, ring),
         out_shape=(
             jax.ShapeDtypeStruct(start.shape, f32),
@@ -251,6 +273,7 @@
         ),
         name="chebyshev",
     )(*(pltpu.with_memory_space_constraint(x, pltpu.HBM) for x in (start, masses, bond_long, bond_trans)))
+    return flush(last, dens)
 
 
 def solution(mesh):

time: 46.7 us -> 46.2 us (0.989)
  local copies, waits for them, and re-layouts: 1.67 us -> 0 us
  Pallas kernels: 44.3 us -> 45.5 us
    unnamed x2 -> x0, local copies, waits for them, and re-layouts: 1.67 us -> none
    pallas_call x0 -> x1, Pallas kernels: none -> 1.1 us  [flush(): pl.pallas_call(flush_kernel, out_shape=tuple((jax.ShapeDtypeStruct(x.shap...]
where the time goes in v3:
time: 46.2 us; the launch traced here: 46.1 us
  Pallas kernels  45.5 us (98%)
  between operations  0.64 us (1%)
    pallas_call x1, Pallas kernels, on_device(): pl.pallas_call(functools.partial(kernel, ring), out_shape=(jax.ShapeDtype...  44.4 us
    pallas_call x1, Pallas kernels, flush(): pl.pallas_call(flush_kernel, out_shape=tuple((jax.ShapeDtypeStruct(x.shap...  1.1 us

profile of v3, /device:TPU:0, one launch (start us, length us, event | category | flops | bytes accessed | tf_op | source)
XLA Modules:
  0.0 46.1 jit_solution(11271511913226431880)
XLA Ops:
  0.6 44.4 %chebyshev.1 = (f32[2,2,3,2,64,128]{5,4,3,2,1,0:T(8,128)S(1)}, f32[4,2,2,64,128]{4,3,2,1,0:T(8,128)S(1)}) custom-call(f32[2,2,3,2,64,128]{5,4,3,2,1,0:T(8,128)} %start_hbm.1, f32[2,2,64,128]{3,2,1,0:T(8,128)} %mass_hbm.1, f32[4,2,64,128]{3,2,1,0:T(8,128)} %long_hbm.1, f32[4,2,64,128]{3,2,1,0:T(8,128)} %trans_hbm.1), custom_call_target="tpu_custom_call" | custom-call | tf_op jit(solution)/shard_map/chebyshev/pallas_call | solution.py:249
  45.0 1.1 %flush.1 = (f32[2,2,3,2,64,128]{5,4,3,2,1,0:T(8,128)}, f32[4,2,2,64,128]{4,3,2,1,0:T(8,128)}) custom-call(f32[2,2,3,2,64,128]{5,4,3,2,1,0:T(8,128)S(1)} %get-tuple-element.4.last_in, f32[4,2,2,64,128]{4,3,2,1,0:T(8,128)S(1)} %get-tuple-element.5.dens_in), custom_call_target="tpu_custom_call" | custom-call | tf_op jit(solution)/shard_map/flush/pallas_call | solution.py:231

commit v4 on v3

--- a/solution.py
+++ b/solution.py
@@ -190,9 +190,6 @@
     for n in range(STEPS):
         for v in range(vecs):
             row_copy(n, v).wait_recv()
-            for plane in range(planes - 1):
-                update(n, v, 0, plane + 1)
-                update(n, v, 1, plane)
             x_copy(n, v, 0).wait_recv()
             update(n, v, 0, 0)
             if n < STEPS - 1:
@@ -206,6 +203,10 @@
             update(n, v, 1, planes - 1)
             if n < STEPS - 1:
                 x_copy(n + 1, v, 0).start()
+            for plane in range(planes - 1):
+                update(n, v, 0, plane + 1)
+                update(n, v, 1, plane)
+            if n < STEPS - 1:
                 row_copy(n + 1, v).start()
 
     for n in range(STEPS):

time: 46.2 us -> 46.4 us (level)
  no operation moved by 1% of the time
where the time goes in v4:
time: 46.4 us; the launch traced here: 46.3 us
  Pallas kernels  45.6 us (98%)
  between operations  0.64 us (1%)
    pallas_call x1, Pallas kernels, on_device(): pl.pallas_call(functools.partial(kernel, ring), out_shape=(jax.ShapeDtype...  44.5 us
    pallas_call x1, Pallas kernels, flush(): pl.pallas_call(flush_kernel, out_shape=tuple((jax.ShapeDtypeStruct(x.shap...  1.1 us

profile of v4, /device:TPU:0, one launch (start us, length us, event | category | flops | bytes accessed | tf_op | source)
XLA Modules:
  0.0 46.3 jit_solution(17803914111713602186)
XLA Ops:
  0.6 44.5 %chebyshev.1 = (f32[2,2,3,2,64,128]{5,4,3,2,1,0:T(8,128)S(1)}, f32[4,2,2,64,128]{4,3,2,1,0:T(8,128)S(1)}) custom-call(f32[2,2,3,2,64,128]{5,4,3,2,1,0:T(8,128)} %start_hbm.1, f32[2,2,64,128]{3,2,1,0:T(8,128)} %mass_hbm.1, f32[4,2,64,128]{3,2,1,0:T(8,128)} %long_hbm.1, f32[4,2,64,128]{3,2,1,0:T(8,128)} %trans_hbm.1), custom_call_target="tpu_custom_call" | custom-call | tf_op jit(solution)/shard_map/chebyshev/pallas_call | solution.py:250
  45.2 1.1 %flush.1 = (f32[2,2,3,2,64,128]{5,4,3,2,1,0:T(8,128)}, f32[4,2,2,64,128]{4,3,2,1,0:T(8,128)}) custom-call(f32[2,2,3,2,64,128]{5,4,3,2,1,0:T(8,128)S(1)} %get-tuple-element.4.last_in, f32[4,2,2,64,128]{4,3,2,1,0:T(8,128)S(1)} %get-tuple-element.5.dens_in), custom_call_target="tpu_custom_call" | custom-call | tf_op jit(solution)/shard_map/flush/pallas_call | solution.py:232
